TPU v7x, 128 devices: a whole 4x4x4 slice. The times are simulated.
128 devices in a mesh: dp: 4 (over x), expert: 32 (over z, y, core).
Axes of the slice: x: 4, y: 4, z: 4, core: 2. Of those that a mesh axis runs over, the one named last changes fastest.
Arguments:
- tokens: bfloat16 [16384, 7168], P(('dp', 'expert')), may hold values from -6 to 6
- cotangents: bfloat16 [16384, 8, 2048], P(('dp', 'expert')), may hold values from -6 to 6
- routing: int32 [16384, 8], P(('dp', 'expert')), may hold values from 0 to 127, all different within a row; in each aligned block of 128 rows (0 to 127, 128 to 255, ...) at most 9 rows name the same one
- sketch_matrix: bfloat16 [64, 7168], replicated, may hold values from -6 to 6
Outputs:
- basis: bfloat16 [128, 64, 2048], P('expert', None, 'dp')
- adapter: float32 [128, 64, 7168], P('expert', None, 'dp')
Inputs may be any that keep to these rules, and one draw needn't show every extreme that they name: `routing`: each row names 8 different experts. Among the 128 rows of one device no expert is named more than 9 times, and in every draw some expert is named exactly 9 times by the rows of some device. Every expert is named by at least 64 rows in all.
All inputs are finite; a program needn't handle non-finite values.
Results may differ from a plain program's by a relative error of at most 0.04.
Values may be sent and summed in bfloat16 or wider, within the bound.
No kernel may reach another device: no remote copies, remote signals or barrier semaphores. Data moves between devices by JAX's collectives and lax.ppermute only.
A program may use at most 192 MiB of HBM per device.

v0:
```python
import math

import jax
import jax.numpy as jnp
from jax import lax
from jax.sharding import PartitionSpec as P

D = 7168
FF = 2048
TOP = 8
EXP_DEV = 4
POWER = 2
TOK_DEV = 128


RIDGE_SHIFT = 0.0001


def slot_table(flat_ids, experts, capacity):
    routed_count = flat_ids.shape[0]
    onehot = (flat_ids[:, None] == jnp.arange(experts, dtype=jnp.int32)[None, :]).astype(jnp.int32)
    before = jnp.cumsum(onehot, axis=0) - onehot
    position = jnp.sum(before * onehot, axis=1)
    target = flat_ids * capacity + position
    vacant = jnp.full((experts * capacity,), -1, jnp.int32)
    return vacant.at[target].set(jnp.arange(routed_count, dtype=jnp.int32))


def gram_of(sketch):
    return jnp.einsum("erf,esf->ers", sketch, sketch, precision=lax.Precision.HIGHEST) / FF


def lower_factor(gram_matrix):
    rank_size = gram_matrix.shape[-1]
    diag_sum = jnp.trace(gram_matrix, axis1=1, axis2=2)
    shifted = gram_matrix + (RIDGE_SHIFT * diag_sum / rank_size)[:, None, None] * jnp.eye(
        rank_size, dtype=jnp.float32
    )
    return jnp.linalg.cholesky(shifted)


def solve_rows(factor, sketch):
    return lax.linalg.triangular_solve(factor, sketch, left_side=True, lower=True)


def shards(tokens, cotangents, routing, sketch_matrix):
    expert_count = lax.axis_size("expert")
    data_count = lax.axis_size("dp")
    experts = EXP_DEV * expert_count
    mean_load = TOK_DEV * TOP // experts
    capacity = mean_load + max(1, TOK_DEV * TOP // (8 * experts))
    routed = TOK_DEV * data_count * TOP // EXP_DEV
    adapter_scale = 1.0 / math.sqrt(FF * routed)
    feature_share = FF // data_count
    slot_index = slot_table(routing.reshape(-1), experts, capacity)
    present = (slot_index >= 0)[:, None]
    safe_index = jnp.maximum(slot_index, 0)
    token_row = safe_index // TOP
    layout = (expert_count, EXP_DEV, capacity)
    send_tokens = jnp.where(present, tokens[token_row], 0).reshape(layout + (D,))
    send_grads = jnp.where(present, cotangents.reshape(-1, FF)[safe_index], 0).reshape(
        layout + (FF,)
    )
    owner_tokens, owner_grads = (
        lax.all_to_all(send_tokens, "expert", split_axis=0, concat_axis=0, tiled=True),
        lax.all_to_all(send_grads, "expert", split_axis=0, concat_axis=0, tiled=True),
    )
    sketch_rows = jnp.einsum(
        "secd,rd->secr", owner_tokens, sketch_matrix, preferred_element_type=jnp.float32
    ).astype(jnp.bfloat16)
    column_start = lax.axis_index("dp") * feature_share
    for iteration in range(POWER + 1):
        sketch = jnp.einsum(
            "secr,secf->erf", sketch_rows, owner_grads, preferred_element_type=jnp.float32
        )
        summed = lax.psum(sketch.astype(jnp.bfloat16), "dp").astype(jnp.float32)
        basis_full = solve_rows(lower_factor(gram_of(summed)), summed).astype(jnp.bfloat16)
        basis_share = lax.dynamic_slice_in_dim(basis_full, column_start, feature_share, 2)
        projected = jnp.einsum(
            "erf,secf->secr", basis_full, owner_grads, preferred_element_type=jnp.float32
        ).astype(jnp.bfloat16)
        partial_value = (
            jnp.einsum(
                "secr,secd->erd", projected, owner_tokens, preferred_element_type=jnp.float32
            )
            * adapter_scale
        )
        if iteration < POWER:
            coefficient = lax.psum(partial_value.astype(jnp.bfloat16), "dp")
            sketch_rows = jnp.einsum(
                "secd,erd->secr", owner_tokens, coefficient, preferred_element_type=jnp.float32
            ).astype(jnp.bfloat16)
    adapter = lax.psum_scatter(
        partial_value.astype(jnp.bfloat16), "dp", scatter_dimension=2, tiled=True
    ).astype(jnp.float32)
    return (basis_share, adapter)


def solution(mesh):
    in_specs = (
        P(("dp", "expert"), None),
        P(("dp", "expert"), None, None),
        P(("dp", "expert"), None),
        P(),
    )
    out_specs = (P("expert", None, "dp"), P("expert", None, "dp"))
    return jax.shard_map(shards, mesh=mesh, in_specs=in_specs, out_specs=out_specs, check_vma=False)
```

profile of v0, /device:TPU:98, one launch (start us, length us, event | category | flops | bytes accessed | tf_op | source)
XLA Modules:
  0.0 999.7 jit_solution(1961235858218972724)
XLA Ops:
  14.5 13.5 %gather_fusion.1 = bf16[1152,7168]{1,0:T(8,128)(2,1)} fusion(bf16[128,7168]{1,0:T(8,128)(2,1)S(1)} %copy-done, s32[2048]{0:T(1024)S(1)} %get-tuple-element.12), kind=kCustom, calls=%fused_computation.1 | custom fusion | bytes 33034752 | tf_op jit(solution)/shard_map/gather | solution.py:60
  27.9 21.5 %gather.13 = bf16[32,4,9,7168]{3,2,1,0:T(8,128)(2,1)} reshape(bf16[1152,7168]{1,0:T(8,128)(2,1)} %gather_fusion.1) | data formatting | bytes 33030144 | tf_op jit(solution)/shard_map/gather | solution.py:60
  49.6 20.2 %broadcast_select_fusion = bf16[32,4,9,7168]{3,2,1,0:T(8,128)(2,1)} fusion(bf16[32,4,9,7168]{3,2,1,0:T(8,128)(2,1)} %gather.13, pred[32,4,9]{2,1,0:T(4,128)(4,1)S(1)} %broadcast_in_dim.66), kind=kLoop, calls=%fused_computation.3 | loop fusion | flops 8257536 | bytes 33031296 | tf_op jit(solution)/shard_map/jit(_where)/select_n | solution.py:60
  69.8 21.8 %copy.89 = bf16[32,4,9,7168]{3,1,2,0:T(4,128)(2,1)} copy(bf16[32,4,9,7168]{3,2,1,0:T(8,128)(2,1)} %broadcast_select_fusion) | data formatting | bytes 33030144 | tf_op jit(solution)/shard_map/jit(_where)/select_n | solution.py:60
  91.6 8.1 all-to-all-start.1
  99.7 13.4 %gather_fusion = bf16[1152,2048]{1,0:T(8,128)(2,1)} fusion(bf16[1024,2048]{1,0:T(8,128)(2,1)} %bitcast.136, s32[2048]{0:T(1024)S(1)} %get-tuple-element.13), kind=kCustom, calls=%fused_computation | custom fusion | bytes 9441792 | tf_op jit(solution)/shard_map/gather | solution.py:61
  113.1 8.0 gather.11
  128.4 10.4 %copy.88 = bf16[32,4,9,2048]{3,1,2,0:T(4,128)(2,1)} copy(bf16[32,4,9,2048]{3,2,1,0:T(8,128)(2,1)} %broadcast_select_fusion.1) | data formatting | bytes 9437184 | tf_op jit(solution)/shard_map/jit(_where)/select_n | solution.py:61
  138.8 161.3 %all-to-all-done.1 = bf16[32,4,9,7168]{3,1,2,0:T(4,128)(2,1)} async-done(((bf16[32,4,9,7168]{3,1,2,0:T(4,128)(2,1)}), bf16[32,4,9,7168]{3,1,2,0:T(4,128)(2,1)}, u32[]{:S(2)}, u32[]{:S(2)}) %all-to-all-start.1) | async-done | bytes 16515104 | tf_op jit(solution)/shard_map/all_to_all | solution.py:65
  300.0 14.5 %all-to-all-start = ((bf16[32,4,9,2048]{3,1,2,0:T(4,128)(2,1)}), bf16[32,4,9,2048]{3,1,2,0:T(4,128)(2,1)}, u32[]{:S(2)}, u32[]{:S(2)}) async-start(bf16[32,4,9,2048]{3,1,2,0:T(4,128)(2,1)} %copy.88), calls=%async_computation | async-start | bytes 9437184 | tf_op jit(solution)/shard_map/all_to_all | solution.py:66
  314.7 14.2 %fusion.43 = bf16[32,4,9,64]{3,0,2,1:T(8,128)(2,1)S(1)} fusion(bf16[32,4,9,7168]{3,1,2,0:T(4,128)(2,1)} %all-to-all-done.1, bf16[64,7168]{1,0:T(8,128)(2,1)S(1)} %copy-done.2), kind=kOutput, calls=%fused_computation.51 | convolution fusion | flops 1057038336 | bytes 17580032 | tf_op jit(solution)/shard_map/secd,rd->secr/dot_general | solution.py:68
  328.9 42.0 %all-to-all-done = bf16[32,4,9,2048]{3,1,2,0:T(4,128)(2,1)} async-done(((bf16[32,4,9,2048]{3,1,2,0:T(4,128)(2,1)}), bf16[32,4,9,2048]{3,1,2,0:T(4,128)(2,1)}, u32[]{:S(2)}, u32[]{:S(2)}) %all-to-all-start) | async-done | bytes 4718624 | tf_op jit(solution)/shard_map/all_to_all | solution.py:66
  370.9 8.8 fusion.17
  379.8 44.7 %all-reduce.6.cloned.1.call-done = bf16[4,64,2048]{2,1,0:T(8,128)(2,1)} async-done(((bf16[4,64,2048]{2,1,0:T(8,128)(2,1)}), bf16[4,64,2048]{2,1,0:T(8,128)(2,1)}) %all-reduce.6.cloned.1.call-update) | async-done | bytes 1048592 | tf_op jit(solution)/shard_map/psum | solution.py:76
  426.9 23.5 %custom-call.10 = f32[4,64,64]{2,1,0:T(8,128)S(1)} custom-call(f32[4,64,64]{2,1,0:T(8,128)S(1)} %fusion.87), custom_call_target="Cholesky" | custom-call | tf_op jit(solution)/shard_map/jit(cholesky)/cholesky | solution.py:39
  450.6 20.1 %custom-call.11 = f32[4,1,64,64]{2,3,1,0:T(8,128)S(1)} custom-call(f32[4,1,64,64]{3,2,1,0:T(8,128)S(1)} %select_bitcast_fusion.2), custom_call_target="InvertDiagBlocksLowerTriangular" | custom-call | tf_op jit(solution)/shard_map/triangular_solve/custom-call.0 | solution.py:43
  478.8 17.6 %fusion.3 = bf16[4,64,7168]{2,1,0:T(8,128)(2,1)} fusion(bf16[32,4,9,64]{3,0,2,1:T(8,128)(2,1)S(1)} %fusion.69, bf16[32,4,9,7168]{3,1,2,0:T(4,128)(2,1)} %all-to-all-done.1), kind=kOutput, calls=%fused_computation.10 | convolution fusion | flops 1060634624 | bytes 20332544 | tf_op jit(solution)/shard_map/secr,secd->erd/dot_general | solution.py:83
  496.6 84.9 %all-reduce.8.cloned.1.call-done = bf16[4,64,7168]{2,1,0:T(8,128)(2,1)} async-done(((bf16[4,64,7168]{2,1,0:T(8,128)(2,1)}), bf16[4,64,7168]{2,1,0:T(8,128)(2,1)}) %all-reduce.8.cloned.1.call-update) | async-done | bytes 3670032 | tf_op jit(solution)/shard_map/psum | solution.py:89
  581.4 13.4 %fusion.61 = bf16[32,4,9,64]{3,0,2,1:T(8,128)(2,1)S(1)} fusion(bf16[32,4,9,7168]{3,1,2,0:T(4,128)(2,1)} %all-to-all-done.1, bf16[4,64,7168]{2,1,0:T(8,128)(2,1)} %all-reduce.8.cloned.1.call-done), kind=kOutput, calls=%fused_computation.55 | convolution fusion | flops 1057038336 | bytes 20332544 | tf_op jit(solution)/shard_map/secd,erd->secr/dot_general | solution.py:90
  594.9 8.8 fusion.18
  603.7 46.0 %all-reduce.10.cloned.1.call-done = bf16[4,64,2048]{2,1,0:T(8,128)(2,1)} async-done(((bf16[4,64,2048]{2,1,0:T(8,128)(2,1)}), bf16[4,64,2048]{2,1,0:T(8,128)(2,1)}) %all-reduce.10.cloned.1.call-update) | async-done | bytes 1048592 | tf_op jit(solution)/shard_map/psum | solution.py:76
  652.1 23.5 %custom-call.12 = f32[4,64,64]{2,1,0:T(8,128)S(1)} custom-call(f32[4,64,64]{2,1,0:T(8,128)S(1)} %fusion.85), custom_call_target="Cholesky" | custom-call | tf_op jit(solution)/shard_map/jit(cholesky)/cholesky | solution.py:39
  675.8 20.1 %custom-call.13 = f32[4,1,64,64]{2,3,1,0:T(8,128)S(1)} custom-call(f32[4,1,64,64]{3,2,1,0:T(8,128)S(1)} %select_bitcast_fusion.1), custom_call_target="InvertDiagBlocksLowerTriangular" | custom-call | tf_op jit(solution)/shard_map/triangular_solve/custom-call.0 | solution.py:43
  704.0 17.6 %fusion.4 = bf16[4,64,7168]{2,1,0:T(8,128)(2,1)} fusion(bf16[32,4,9,64]{3,0,2,1:T(8,128)(2,1)S(1)} %fusion.72, bf16[32,4,9,7168]{3,1,2,0:T(4,128)(2,1)} %all-to-all-done.1), kind=kOutput, calls=%fused_computation.11 | convolution fusion | flops 1060634624 | bytes 20332544 | tf_op jit(solution)/shard_map/secr,secd->erd/dot_general | solution.py:83
  721.7 84.9 %all-reduce.12.cloned.1.call-done = bf16[4,64,7168]{2,1,0:T(8,128)(2,1)} async-done(((bf16[4,64,7168]{2,1,0:T(8,128)(2,1)}), bf16[4,64,7168]{2,1,0:T(8,128)(2,1)}) %all-reduce.12.cloned.1.call-update) | async-done | bytes 3670032 | tf_op jit(solution)/shard_map/psum | solution.py:89
  806.6 13.4 %fusion.56 = bf16[32,4,9,64]{3,0,2,1:T(8,128)(2,1)S(1)} fusion(bf16[32,4,9,7168]{3,1,2,0:T(4,128)(2,1)} %all-to-all-done.1, bf16[4,64,7168]{2,1,0:T(8,128)(2,1)} %all-reduce.12.cloned.1.call-done), kind=kOutput, calls=%fused_computation.54 | convolution fusion | flops 1057038336 | bytes 20332544 | tf_op jit(solution)/shard_map/secd,erd->secr/dot_general | solution.py:90
  820.1 8.8 fusion.19
  828.9 46.0 %all-reduce.14.cloned.1.call-done = bf16[4,64,2048]{2,1,0:T(8,128)(2,1)} async-done(((bf16[4,64,2048]{2,1,0:T(8,128)(2,1)}), bf16[4,64,2048]{2,1,0:T(8,128)(2,1)}) %all-reduce.14.cloned.1.call-update) | async-done | bytes 1048592 | tf_op jit(solution)/shard_map/psum | solution.py:76
  877.3 23.5 %custom-call.14 = f32[4,64,64]{2,1,0:T(8,128)S(1)} custom-call(f32[4,64,64]{2,1,0:T(8,128)S(1)} %fusion.83), custom_call_target="Cholesky" | custom-call | tf_op jit(solution)/shard_map/jit(cholesky)/cholesky | solution.py:39
  901.0 19.9 %custom-call.15 = f32[4,1,64,64]{2,3,1,0:T(8,128)S(1)} custom-call(f32[4,1,64,64]{3,2,1,0:T(8,128)S(1)} %select_bitcast_fusion), custom_call_target="InvertDiagBlocksLowerTriangular" | custom-call | tf_op jit(solution)/shard_map/triangular_solve/custom-call.0 | solution.py:43
  929.0 17.9 %fusion.5 = bf16[4,64,7168]{2,1,0:T(8,128)(2,1)} fusion(bf16[32,4,9,64]{3,0,2,1:T(8,128)(2,1)S(1)} %fusion.66, bf16[32,4,9,7168]{3,1,2,0:T(4,128)(2,1)} %all-to-all-done.1), kind=kOutput, calls=%fused_computation.12 | convolution fusion | flops 1060634624 | bytes 20332544 | tf_op jit(solution)/shard_map/secr,secd->erd/dot_general | solution.py:83
  947.7 42.3 %reduce-scatter.2.cloned.1.call-done = bf16[4,64,1792]{2,1,0:T(8,128)(2,1)} async-done(((bf16[4,64,7168]{2,1,0:T(8,128)(2,1)}), bf16[4,64,1792]{2,1,0:T(8,128)(2,1)}) %reduce-scatter.2.cloned.1.call-update) | async-done | bytes 917520 | tf_op jit(solution)/shard_map/reduce_scatter | solution.py:93
  (76 shorter events, 50.7 us)
Async XLA Ops:
  7.2 7.3 copy-start
  91.6 208.4 %all-to-all-start.1 = ((bf16[32,4,9,7168]{3,1,2,0:T(4,128)(2,1)}), bf16[32,4,9,7168]{3,1,2,0:T(4,128)(2,1)}, u32[]{:S(2)}, u32[]{:S(2)}) async-start(bf16[32,4,9,7168]{3,1,2,0:T(4,128)(2,1)} %copy.89), calls=%async_computation.1 | async-start | bytes 33030144 | tf_op jit(solution)/shard_map/all_to_all | solution.py:65
  138.7 176.0 %copy-start.2 = (bf16[64,7168]{1,0:T(8,128)(2,1)S(1)}, bf16[64,7168]{1,0:T(8,128)(2,1)}, u32[]{:S(2)}) copy-start(bf16[64,7168]{1,0:T(8,128)(2,1)} %param.10) | copy-start | bytes 2752516
  300.0 70.9 %all-to-all-start = ((bf16[32,4,9,2048]{3,1,2,0:T(4,128)(2,1)}), bf16[32,4,9,2048]{3,1,2,0:T(4,128)(2,1)}, u32[]{:S(2)}, u32[]{:S(2)}) async-start(bf16[32,4,9,2048]{3,1,2,0:T(4,128)(2,1)} %copy.88), calls=%async_computation | async-start | bytes 9437184 | tf_op jit(solution)/shard_map/all_to_all | solution.py:66
  314.5 110.1 %all-reduce.6.cloned.1.call-start = ((), (), s32[]{:S(2)}) async-start(), calls=%async_computation.3 | async-start | bytes 2097152 | tf_op jit(solution)/shard_map/psum | solution.py:76
  379.7 201.7 %all-reduce.8.cloned.1.call-start = ((), (), s32[]{:S(2)}) async-start(), calls=%async_computation.4 | async-start | bytes 7340032 | tf_op jit(solution)/shard_map/psum | solution.py:89
  496.5 153.2 %all-reduce.10.cloned.1.call-start = ((), (), s32[]{:S(2)}) async-start(), calls=%async_computation.5 | async-start | bytes 2097152 | tf_op jit(solution)/shard_map/psum | solution.py:76
  603.7 202.9 %all-reduce.12.cloned.1.call-start = ((), (), s32[]{:S(2)}) async-start(), calls=%async_computation.6 | async-start | bytes 7340032 | tf_op jit(solution)/shard_map/psum | solution.py:89
  721.7 153.2 %all-reduce.14.cloned.1.call-start = ((), (), s32[]{:S(2)}) async-start(), calls=%async_computation.7 | async-start | bytes 2097152 | tf_op jit(solution)/shard_map/psum | solution.py:76
  828.8 161.2 %reduce-scatter.2.cloned.1.call-start = ((), (), s32[]{:S(2)}) async-start(), calls=%async_computation.8 | async-start | bytes 4587520 | tf_op jit(solution)/shard_map/reduce_scatter | solution.py:93
  929.0 63.6 %copy-start.1 = (bf16[128,7168]{1,0:T(8,128)(2,1)S(1)}, bf16[128,7168]{1,0:T(8,128)(2,1)}, u32[]{:S(2)}) copy-start(bf16[128,7168]{1,0:T(8,128)(2,1)} %param.7) | copy-start | bytes 5505028
Sparse Core Ops, SparseCore 0:
  379.8 44.6 all-reduce.5
  496.6 84.7 all-reduce.7
  603.8 45.8 all-reduce.9
  721.8 84.7 all-reduce.11
  829.0 45.8 all-reduce.13
  947.1 42.9 reduce-scatter.1
where the time goes:
time: 1010 us; the launch traced here: 1000 us
  waiting for transfers between devices  552 us (55%)
  other arithmetic  163 us (16%)
  matrix products  151 us (15%)
  local copies, waits for them, and re-layouts  95.6 us (9%)
  starting transfers between devices  23 us (2%)
  between operations  14.7 us (1%)
    psum x2, waiting for transfers between devices, shards(): coefficient = lax.psum(partial_value.astype(jnp.bfloat16), 'dp')  170 us
    all_to_all x1, waiting for transfers between devices, shards(): lax.all_to_all(send_tokens, 'expert', split_axis=0, concat_axis=0, tiled=...  161 us
    psum x3, waiting for transfers between devices, shards(): summed = lax.psum(sketch.astype(jnp.bfloat16), 'dp').astype(jnp.float32)  137 us
    another operation x10, other arithmetic, lower_factor(): return jnp.linalg.cholesky(shifted)  70.8 us
    another operation x7, other arithmetic, solve_rows(): lax.linalg.triangular_solve(factor, sketch, left_side=True, lower=True)  60.3 us
    dot_general x3, matrix products, shards(): jnp.einsum('secr,secd->erd', projected, owner_tokens, preferred_element_t...  53.2 us
    reduce_scatter x1, waiting for transfers between devices, shards(): lax.psum_scatter(partial_value.astype(jnp.bfloat16), 'dp', scatter_dimens...  42.3 us
    all_to_all x1, waiting for transfers between devices, shards(): lax.all_to_all(send_grads, 'expert', split_axis=0, concat_axis=0, tiled=T...  42 us
  transfers between devices with their start and end apart: 8, of which 8 were waited for; matrix products, arithmetic and copies ran while one was open for 5% of the time, Pallas kernels for 0%

commit v1 on v0

v1 whole, which is shorter than its diff:
```python
import functools
import math

import jax
import jax.numpy as jnp
from jax import lax
from jax.experimental import pallas as pl
from jax.experimental.pallas import tpu as pltpu
from jax.sharding import PartitionSpec as P

D = 7168
FF = 2048
RANK = 64
TOP = 8
POWER = 2
TOK_DEV = 128
EXPERTS = 128
ROUTED = 1024
SLOTS = 8
ROWS = EXPERTS * SLOTS
FOLD_D = D // SLOTS
FOLD_FF = FF // SLOTS
G_WIDTH = FF + FOLD_FF + 128
X_WIDTH = D + FOLD_D
RIDGE_SHIFT = 0.0001
SCALE = 1.0 / math.sqrt(FF * ROUTED)
VMEM = 56 * 1024 * 1024
F32 = jnp.float32
BF16 = jnp.bfloat16
HIGHEST = lax.Precision.HIGHEST


def dot(a, b, contract, precision=None):
    return lax.dot_general(
        a, b, ((contract[:1], contract[1:]), ((), ())), precision=precision, preferred_element_type=F32
    )


def iota(shape, axis):
    return lax.broadcasted_iota(jnp.int32, shape, axis)


def ones_where(mask):
    return jnp.where(mask, 1.0, 0.0).astype(F32).astype(BF16)


def pack_grads_kernel(flat_ref, by_choice_ref, tok_ref, sketch_ref, cot_ref, out_ref, sel_ref, fold_ref, tail_ref):
    square = (EXPERTS, TOK_DEV)
    owner = iota(square, 0)
    named = jnp.zeros(square, F32)
    for k in range(TOP):
        named = named + jnp.where(by_choice_ref[k : k + 1, :] == owner, 1.0, 0.0)
    earlier = ones_where(iota(square, 0) < iota(square, 1))
    before = dot(named.astype(BF16), earlier, (1, 0))
    slot = jnp.where(named > 0.0, before, -1.0)
    spread = ones_where(iota((ROWS, EXPERTS), 0) // SLOTS == iota((ROWS, EXPERTS), 1))
    row_slot = dot(spread, slot.astype(BF16), (1, 0))
    sel = ones_where(row_slot == (iota((ROWS, TOK_DEV), 0) % SLOTS).astype(F32))
    sel_last = ones_where(slot == float(SLOTS))
    sel_ref[:ROWS, :] = sel
    sel_ref[ROWS:, :] = sel_last
    sketched = dot(tok_ref[...], sketch_ref[...], (1, 1)).astype(BF16)
    tail_ref[:, :RANK] = dot(sel, sketched, (1, 0))
    tail_ref[:, RANK:] = jnp.zeros((ROWS, 128 - RANK), F32)
    last_rows = dot(sel_last, sketched, (1, 0))
    tail_ref[pl.ds(0, EXPERTS, stride=SLOTS), :] = jnp.concatenate(
        [tail_ref[pl.ds(0, EXPERTS, stride=SLOTS), :][:, :RANK], last_rows], axis=1
    )
    out_ref[:, FF + FOLD_FF :] = tail_ref[...].astype(BF16)
    pairs = (TOK_DEV, TOK_DEV * TOP)
    token_of = ones_where(iota(pairs, 1) // TOP == iota(pairs, 0))
    flat = flat_ref[...]
    whole = (ROWS, TOK_DEV * TOP)
    sel_pair = ones_where((dot(sel, token_of, (1, 0)) > 0.5) & (iota(whole, 0) // SLOTS == flat))
    out_ref[:, :FF] = dot(sel_pair, cot_ref[...], (1, 0)).astype(BF16)
    last_pair = ones_where((dot(sel_last, token_of, (1, 0)) > 0.5) & (iota((EXPERTS, ROWS), 0) == flat))
    last = dot(last_pair, cot_ref[...], (1, 0))
    for r in range(SLOTS):
        for h in range(FOLD_FF // 128):
            c = r * FOLD_FF + h * 128
            fold_ref[h, pl.ds(r, EXPERTS, stride=SLOTS), :] = last[:, c : c + 128]
    for h in range(FOLD_FF // 128):
        out_ref[:, FF + h * 128 : FF + (h + 1) * 128] = fold_ref[h].astype(BF16)


def pack_grads(flat, by_choice, tokens, sketch_matrix, cot):
    return pl.pallas_call(
        pack_grads_kernel,
        out_shape=(
            jax.ShapeDtypeStruct((ROWS, G_WIDTH), BF16),
            jax.ShapeDtypeStruct((ROWS + EXPERTS, TOK_DEV), BF16),
        ),
        scratch_shapes=[pltpu.VMEM((FOLD_FF // 128, ROWS, 128), F32), pltpu.VMEM((ROWS, 128), F32)],
        compiler_params=pltpu.CompilerParams(vmem_limit_bytes=VMEM),
        cost_estimate=pl.CostEstimate(flops=2 * ROWS * ROWS * FF, bytes_accessed=14_000_000, transcendentals=0),
        name="pack_grads",
    )(flat, by_choice, tokens, sketch_matrix, cot)


def pack_tokens_kernel(sel_ref, tok_ref, out_ref, fold_ref):
    step = pl.program_id(0)

    @pl.when(step < SLOTS)
    def _():
        out_ref[...] = dot(sel_ref[:ROWS, :], tok_ref[...], (1, 0)).astype(BF16)
        last = dot(sel_ref[ROWS:, :], tok_ref[...], (1, 0))
        for h in range(FOLD_D // 128):
            fold_ref[h, pl.ds(step, EXPERTS, stride=SLOTS), :] = last[:, h * 128 : (h + 1) * 128]

    @pl.when(step == SLOTS)
    def _():
        for h in range(FOLD_D // 128):
            out_ref[:, h * 128 : (h + 1) * 128] = fold_ref[h].astype(BF16)


def pack_tokens(sel, tokens):
    return pl.pallas_call(
        pack_tokens_kernel,
        grid=(SLOTS + 1,),
        in_specs=[
            pl.BlockSpec((ROWS + EXPERTS, TOK_DEV), lambda i: (0, 0)),
            pl.BlockSpec((TOK_DEV, FOLD_D), lambda i: (0, jnp.minimum(i, SLOTS - 1))),
        ],
        out_specs=pl.BlockSpec((ROWS, FOLD_D), lambda i: (0, i)),
        out_shape=jax.ShapeDtypeStruct((ROWS, X_WIDTH), BF16),
        scratch_shapes=[pltpu.VMEM((FOLD_D // 128, ROWS, 128), F32)],
        compiler_params=pltpu.CompilerParams(vmem_limit_bytes=VMEM),
        cost_estimate=pl.CostEstimate(flops=2 * ROWS * TOK_DEV * D, bytes_accessed=19_000_000, transcendentals=0),
        name="pack_tokens",
    )(sel, tokens)


def inverse_factor(gram):
    rows, cols = iota((RANK, 2 * RANK), 0), iota((RANK, 2 * RANK), 1)
    diagonal = jnp.where(rows == cols, jnp.concatenate([gram, gram], axis=1), 0.0)
    mean = jnp.sum(jnp.sum(diagonal, axis=1, keepdims=True), axis=0, keepdims=True) / RANK
    unit = jnp.where(cols == rows + RANK, 1.0, 0.0)
    left = jnp.concatenate([gram, jnp.zeros((RANK, RANK), F32)], axis=1)
    work = left + unit + jnp.where(rows == cols, RIDGE_SHIFT * mean, 0.0)
    pivots = jnp.zeros((RANK, 1), F32)
    index = iota((RANK, 1), 0)
    for j in range(RANK):
        row = work[j : j + 1, :]
        pivot = row[:, j : j + 1]
        pivots = jnp.where(index == j, pivot, pivots)
        factor = jnp.where(index > j, work[:, j : j + 1] / pivot, 0.0)
        work = work - factor * row
    return work[:, RANK:] * lax.rsqrt(pivots)


def half_round(rows_main, rows_last, grads, grads_last):
    sketch = dot(rows_main, grads, (1, 0)) + dot(rows_last, grads_last, (1, 0))
    gram = dot(sketch, sketch, (1, 1), HIGHEST) / FF
    basis = dot(inverse_factor(gram), sketch, (1, 0), HIGHEST).astype(BF16)
    return basis, dot(basis, grads, (1, 1)).astype(BF16), dot(basis, grads_last, (1, 1)).astype(BF16)


def first_round_kernel(g_ref, main_ref, last_ref, grads_last_ref, fold_ref):
    for h in range(FOLD_FF // 128):
        fold_ref[h] = g_ref[:, FF + h * 128 : FF + (h + 1) * 128].astype(F32)
    for r in range(SLOTS):
        for h in range(FOLD_FF // 128):
            c = r * FOLD_FF + h * 128
            grads_last_ref[:, c : c + 128] = fold_ref[h, pl.ds(r, EXPERTS, stride=SLOTS), :].astype(BF16)
    fold_ref[0] = g_ref[:, FF + FOLD_FF :].astype(F32)
    tail_t = jnp.transpose(fold_ref[0])
    last_t = jnp.transpose(fold_ref[0, pl.ds(0, EXPERTS, stride=SLOTS), :])
    rows_main = tail_t[:RANK, :].astype(BF16)
    rows_last = last_t[RANK:, :].astype(BF16)
    _, main, last = half_round(rows_main, rows_last, g_ref[:, :FF], grads_last_ref[...])
    main_ref[...] = main
    last_ref[...] = last


def first_round(g):
    return pl.pallas_call(
        first_round_kernel,
        out_shape=(
            jax.ShapeDtypeStruct((RANK, ROWS), BF16),
            jax.ShapeDtypeStruct((RANK, EXPERTS), BF16),
            jax.ShapeDtypeStruct((EXPERTS, FF), BF16),
        ),
        scratch_shapes=[pltpu.VMEM((FOLD_FF // 128, ROWS, 128), F32)],
        compiler_params=pltpu.CompilerParams(vmem_limit_bytes=VMEM),
        cost_estimate=pl.CostEstimate(flops=20_000_000_000, bytes_accessed=6_000_000, transcendentals=0),
        name="first_round",
    )(g)


def power_kernel(x_hbm, g_hbm, main_ref, last_ref, grads_last_ref, basis_ref, adapter_ref, x_ref, x_last_ref, g_ref, fold_ref, sems):
    copies = []
    for i in range(SLOTS + 1):
        span = pl.ds(i * FOLD_D, FOLD_D)
        copies.append(pltpu.make_async_copy(x_hbm.at[:, span], x_ref.at[:, span], sems.at[i]))
    g_copy = pltpu.make_async_copy(g_hbm.at[:, pl.ds(0, FF)], g_ref, sems.at[SLOTS + 1])
    copies[SLOTS].start()
    for i in range(SLOTS):
        copies[i].start()
    g_copy.start()
    copies[SLOTS].wait()
    for h in range(FOLD_D // 128):
        fold_ref[h] = x_ref[:, D + h * 128 : D + (h + 1) * 128].astype(F32)
    for r in range(SLOTS):
        for h in range(FOLD_D // 128):
            c = r * FOLD_D + h * 128
            x_last_ref[:, c : c + 128] = fold_ref[h, pl.ds(r, EXPERTS, stride=SLOTS), :].astype(BF16)
    main, last = main_ref[...], last_ref[...]
    for step in range(POWER):
        rows_main = jnp.zeros((RANK, ROWS), F32)
        rows_last = jnp.zeros((RANK, EXPERTS), F32)
        for i in range(SLOTS):
            if step == 0:
                copies[i].wait()
            span = pl.ds(i * FOLD_D, FOLD_D)
            coefficient = dot(main, x_ref[:, span], (1, 0)) + dot(last, x_last_ref[:, span], (1, 0))
            coefficient = (coefficient * SCALE).astype(BF16)
            rows_main = rows_main + dot(coefficient, x_ref[:, span], (1, 1))
            rows_last = rows_last + dot(coefficient, x_last_ref[:, span], (1, 1))
        if step == 0:
            g_copy.wait()
        basis, main, last = half_round(
            rows_main.astype(BF16), rows_last.astype(BF16), g_ref[...], grads_last_ref[...]
        )
    basis_ref[...] = basis
    for i in range(SLOTS):
        span = pl.ds(i * FOLD_D, FOLD_D)
        adapter = dot(main, x_ref[:, span], (1, 0)) + dot(last, x_last_ref[:, span], (1, 0))
        adapter_ref[:, span] = (adapter * SCALE).astype(BF16)


def power(x, g, main, last, grads_last):
    anywhere, vmem = pl.BlockSpec(memory_space=pl.ANY), pl.BlockSpec(memory_space=pltpu.VMEM)
    return pl.pallas_call(
        power_kernel,
        in_specs=[anywhere, anywhere, vmem, vmem, vmem],
        out_specs=(vmem, vmem),
        out_shape=(jax.ShapeDtypeStruct((RANK, FF), BF16), jax.ShapeDtypeStruct((RANK, D), BF16)),
        scratch_shapes=[
            pltpu.VMEM((ROWS, X_WIDTH), BF16),
            pltpu.VMEM((EXPERTS, D), BF16),
            pltpu.VMEM((ROWS, FF), BF16),
            pltpu.VMEM((FOLD_D // 128, ROWS, 128), F32),
            pltpu.SemaphoreType.DMA((SLOTS + 2,)),
        ],
        compiler_params=pltpu.CompilerParams(vmem_limit_bytes=VMEM),
        cost_estimate=pl.CostEstimate(flops=40_000_000_000, bytes_accessed=24_000_000, transcendentals=0),
        name="power",
    )(x, g, main, last, grads_last)


def shards(tokens, cotangents, routing, sketch_matrix):
    groups = lax.axis_size("expert")
    everyone = ("dp", "expert")
    per_group = EXPERTS // groups
    owner = (routing % per_group) * groups + routing // per_group
    g_send, sel = pack_grads(
        owner.reshape(1, -1), owner.T, tokens, sketch_matrix, cotangents.reshape(TOK_DEV * TOP, FF)
    )
    x_send = pack_tokens(sel, tokens)
    swap = lambda v: lax.all_to_all(
        v.reshape(EXPERTS, SLOTS, v.shape[1]), everyone, split_axis=0, concat_axis=0, tiled=True
    ).reshape(v.shape)
    g = swap(g_send)
    x_send, g = lax.optimization_barrier((x_send, g))
    x = swap(x_send)
    main, last, grads_last = first_round(g)
    basis, adapter = power(x, g, main, last, grads_last)
    data = lax.axis_size("dp")
    both = jnp.concatenate(
        [adapter.reshape(RANK, data, -1), basis.reshape(RANK, data, -1)], axis=2
    ).transpose(1, 0, 2)
    both = lax.all_to_all(both, "dp", split_axis=0, concat_axis=0, tiled=True)
    width = D // data
    return both[:, :, width:], both[:, :, :width].astype(F32)


def solution(mesh):
    in_specs = (
        P(("dp", "expert"), None),
        P(("dp", "expert"), None, None),
        P(("dp", "expert"), None),
        P(),
    )
    out_specs = (P("expert", None, "dp"), P("expert", None, "dp"))
    return jax.shard_map(shards, mesh=mesh, in_specs=in_specs, out_specs=out_specs, check_vma=False)
```

time: 1010 us -> 414 us (0.41)
  waiting for transfers between devices: 552 us -> 281 us
  other arithmetic: 163 us -> 3.43 us
  matrix products: 151 us -> 0 us
  local copies, waits for them, and re-layouts: 95.6 us -> 2.83 us
  Pallas kernels: 0 us -> 81.6 us
  blocking collectives: 0 us -> 17.9 us
  between operations: 14.7 us -> 1.14 us
    psum x5 -> x0, waiting for transfers between devices: 306 us -> none  [the longest x2 170 us: shards(): coefficient = lax.psum(partial_value.astype(jnp.bfloat16), 'dp')]
    dot_general x15 -> x0, matrix products: 142 us -> none  [the longest x3 53.2 us: shards(): jnp.einsum('secr,secd->erd', projected, owner_tokens, preferred_element_t...]
    another operation x20 -> x0, other arithmetic: 131 us -> none  [the longest x10 70.8 us: lower_factor(): return jnp.linalg.cholesky(shifted)]
    pallas_call x0 -> x4, Pallas kernels: none -> 81.6 us  [the longest x1 44.3 us: power(): pl.pallas_call(power_kernel, in_specs=[anywhere, anywhere, vmem, vmem, vm...]
    all_to_all x2, waiting for transfers between devices: 203 us -> 281 us  [shards(): lax.all_to_all(v.reshape(EXPERTS, SLOTS, v.shape[1]), everyone, split_axi...]
    gather x4 -> x0, local copies, waits for them, and re-layouts: 56.3 us -> none  [the longest x2 34.9 us: shards(): tokens[token_row]]
    reduce_scatter x1 -> x0, waiting for transfers between devices: 42.3 us -> none  [shards(): lax.psum_scatter(partial_value.astype(jnp.bfloat16), 'dp', scatter_dimens...]
    select_n x2 -> x0, local copies, waits for them, and re-layouts: 32.1 us -> none  [the longest x1 21.8 us: shards(): jnp.where(present, tokens[token_row], 0).reshape(layout + (D,))]
  transfers between devices with their start and end apart: 8 -> 2, of which waited for: 8 -> 2; matrix products, arithmetic and copies ran while one was open for 5% -> 0% of each run, Pallas kernels for 0% -> 6%
where the time goes in v1:
time: 414 us; the launch traced here: 406 us
  waiting for transfers between devices  281 us (68%)
  Pallas kernels  81.6 us (20%)
  starting transfers between devices  18.8 us (5%)
  blocking collectives  17.9 us (4%)
    all_to_all x2, waiting for transfers between devices, shards(): lax.all_to_all(v.reshape(EXPERTS, SLOTS, v.shape[1]), everyone, split_axi...  281 us
    pallas_call x1, Pallas kernels, power(): pl.pallas_call(power_kernel, in_specs=[anywhere, anywhere, vmem, vmem, vm...  44.3 us
    all_to_all x2, starting transfers between devices, shards(): lax.all_to_all(v.reshape(EXPERTS, SLOTS, v.shape[1]), everyone, split_axi...  18.8 us
    all_to_all x1, blocking collectives, shards(): both = lax.all_to_all(both, 'dp', split_axis=0, concat_axis=0, tiled=True)  17.9 us
    pallas_call x1, Pallas kernels, first_round(): pl.pallas_call(first_round_kernel, out_shape=(jax.ShapeDtypeStruct((RANK,...  13.4 us
    pallas_call x1, Pallas kernels, pack_grads(): pl.pallas_call(pack_grads_kernel, out_shape=(jax.ShapeDtypeStruct((ROWS,...  12.7 us
    pallas_call x1, Pallas kernels, pack_tokens(): pl.pallas_call(pack_tokens_kernel, grid=(SLOTS + 1,), in_specs=[pl.BlockS...  11.2 us
  transfers between devices with their start and end apart: 2, of which 2 were waited for; matrix products, arithmetic and copies ran while one was open for 0% of the time, Pallas kernels for 6%

profile of v1, /device:TPU:98, one launch (start us, length us, event | category | flops | bytes accessed | tf_op | source)
XLA Modules:
  0.0 406.3 jit_solution(305012396137291694)
XLA Ops:
  0.6 1.3 fusion.6.by_choice_ref
  1.9 0.7 fusion.1
  2.6 0.1 copy.8
  2.7 0.7 reshape.28.flat_ref
  3.4 12.7 %pack_grads.1 = (bf16[1024,2432]{1,0:T(8,128)(2,1)}, bf16[1152,128]{1,0:T(8,128)(2,1)}) custom-call(s32[1,1024]{1,0:T(1,128)} %reshape.28.flat_ref, s32[8,128]{1,0:T(8,128)} %fusion.6.by_choice_ref, bf16[128,7168]{1,0:T(8,128)(2,1)} %tok_ref.3, bf16[64,7168]{1,0:T(8,128)(2,1)} %sketch_ref.1, bf16[1024,2048]{1,0:T(8,128)(2,1)} %bitcast.23), custom_call_target="tpu_custom_call" | custom-call | flops 4294967296 | bytes 14000000 | tf_op jit(solution)/shard_map/pack_grads/pallas_call | solution.py:87
  16.1 10.2 %all-to-all-start = ((bf16[128,8,2432]{2,1,0:T(8,128)(2,1)}), bf16[128,8,2432]{2,1,0:T(8,128)(2,1)}, u32[]{:S(2)}, u32[]{:S(2)}) async-start(bf16[128,8,2432]{2,1,0:T(8,128)(2,1)} %bitcast.18), calls=%async_computation | async-start | bytes 9961472 | tf_op jit(solution)/shard_map/all_to_all | solution.py:260
  26.4 11.2 %pack_tokens.1 = bf16[1024,8064]{1,0:T(8,128)(2,1)} custom-call(bf16[1152,128]{1,0:T(8,128)(2,1)} %get-tuple-element.11.sel_ref, bf16[128,7168]{1,0:T(8,128)(2,1)} %tok_ref.3), custom_call_target="tpu_custom_call" | custom-call | flops 1879048192 | bytes 19000000 | tf_op jit(solution)/shard_map/pack_tokens/pallas_call | solution.py:117
  37.5 48.3 %all-to-all-done = bf16[128,8,2432]{2,1,0:T(8,128)(2,1)} async-done(((bf16[128,8,2432]{2,1,0:T(8,128)(2,1)}), bf16[128,8,2432]{2,1,0:T(8,128)(2,1)}, u32[]{:S(2)}, u32[]{:S(2)}) %all-to-all-start) | async-done | bytes 4980768 | tf_op jit(solution)/shard_map/all_to_all | solution.py:260
  85.8 8.5 %all-to-all-start.1 = ((bf16[128,8,8064]{2,1,0:T(8,128)(2,1)}), bf16[128,8,8064]{2,1,0:T(8,128)(2,1)}, u32[]{:S(2)}, u32[]{:S(2)}) async-start(bf16[128,8,8064]{2,1,0:T(8,128)(2,1)} %bitcast.17), calls=%async_computation.1 | async-start | bytes 33030144 | tf_op jit(solution)/shard_map/all_to_all | solution.py:260
  94.4 13.4 %first_round.1 = (bf16[64,1024]{1,0:T(8,128)(2,1)}, bf16[64,128]{1,0:T(8,128)(2,1)}, bf16[128,2048]{1,0:T(8,128)(2,1)}) custom-call(bf16[1024,2432]{1,0:T(8,128)(2,1)} %bitcast.3.g_ref.g_hbm), custom_call_target="tpu_custom_call" | custom-call | flops 20000000000 | bytes 6000000 | tf_op jit(solution)/shard_map/first_round/pallas_call | solution.py:176
  107.7 232.4 %all-to-all-done.1 = bf16[128,8,8064]{2,1,0:T(8,128)(2,1)} async-done(((bf16[128,8,8064]{2,1,0:T(8,128)(2,1)}), bf16[128,8,8064]{2,1,0:T(8,128)(2,1)}, u32[]{:S(2)}, u32[]{:S(2)}) %all-to-all-start.1) | async-done | bytes 16515104 | tf_op jit(solution)/shard_map/all_to_all | solution.py:260
  340.1 44.3 %power.1 = (bf16[64,2048]{1,0:T(8,128)(2,1)}, bf16[64,7168]{1,0:T(8,128)(2,1)}) custom-call(bf16[1024,8064]{1,0:T(8,128)(2,1)} %bitcast.5.x_hbm, bf16[1024,2432]{1,0:T(8,128)(2,1)} %bitcast.3.g_ref.g_hbm, bf16[64,1024]{1,0:T(8,128)(2,1)} %get-tuple-element.15.main_ref, bf16[64,128]{1,0:T(8,128)(2,1)} %get-tuple-element.16.last_ref, ...), custom_call_target="tpu_custom_call" | custom-call | flops 40000000000 | bytes 24000000 | tf_op jit(solution)/shard_map/power/pallas_call | solution.py:233
  384.4 0.0 copy-start
  384.5 1.3 copy.15
  385.7 0.0 copy-done
  385.8 0.1 maximum_bitcast_fusion
  385.9 17.9 %all_to_all.15 = bf16[4,64,2304]{2,1,0:T(8,128)(2,1)S(1)} all-to-all(bf16[4,64,2304]{2,1,0:T(8,128)(2,1)S(1)} %maximum_bitcast_fusion), channel_id=1, replica_groups=mesh['dp'=4,'expert'=32] {'dp'}, dimensions={0} | all-to-all | bytes 2359296 | tf_op jit(solution)/shard_map/all_to_all | solution.py:272
  403.8 0.7 slice.8
  404.5 1.4 slice_convert_fusion
  (1 shorter events, 0.0 us)
Async XLA Ops:
  16.1 69.7 %all-to-all-start = ((bf16[128,8,2432]{2,1,0:T(8,128)(2,1)}), bf16[128,8,2432]{2,1,0:T(8,128)(2,1)}, u32[]{:S(2)}, u32[]{:S(2)}) async-start(bf16[128,8,2432]{2,1,0:T(8,128)(2,1)} %bitcast.18), calls=%async_computation | async-start | bytes 9961472 | tf_op jit(solution)/shard_map/all_to_all | solution.py:260
  85.8 254.3 %all-to-all-start.1 = ((bf16[128,8,8064]{2,1,0:T(8,128)(2,1)}), bf16[128,8,8064]{2,1,0:T(8,128)(2,1)}, u32[]{:S(2)}, u32[]{:S(2)}) async-start(bf16[128,8,8064]{2,1,0:T(8,128)(2,1)} %bitcast.17), calls=%async_computation.1 | async-start | bytes 33030144 | tf_op jit(solution)/shard_map/all_to_all | solution.py:260
  384.4 1.3 copy-start
